TPU v7x, 512 devices: a whole 4x4x16 slice. The times are simulated.
512 devices in a mesh: gy: 32 (over z, core), gz: 16 (over y, x).
Axes of the slice: x: 4, y: 4, z: 16, core: 2. Of those that a mesh axis runs over, the one named last changes fastest.
Arguments:
- measured: float32 [16, 1024, 1024], P('gz', 'gy'), may hold values from -20 to 20
- point_spread: float32 [1024, 1024], P('gy'), may hold values from -0.005859375 to 0.005859375
- stencil_weights: float32 [3, 3, 3], replicated, may hold values from -0.9 to 0.9
- upstream: float32 [16, 1024, 1024], P('gz', 'gy'), may hold values from -6 to 6
Outputs:
- grad_measured: float32 [16, 1024, 1024], P('gz', 'gy')
- grad_stencil: float32 [3, 3, 3], replicated
All inputs are finite; a program needn't handle non-finite values.
Results may differ from a plain program's by a relative error of at most 0.00021.
Values sent between devices are 32-bit elements; how exact they have to be, the bound alone decides.
No kernel may reach another device: no remote copies, remote signals or barrier semaphores. Data moves between devices by JAX's collectives and lax.ppermute only.
A program may use at most 64 MiB of HBM per device.

v0:
```python
import math
import jax
import jax.numpy as jnp
from jax import lax
from jax.sharding import Mesh
from jax.sharding import PartitionSpec as P

ITERS = 2
GY = ("gy_0", "gy_1")
GY_GZ = ("gy_0", "gy_1", "gz_0", "gz_1")
GZ = ("gz_0", "gz_1")
highest = lax.Precision.HIGHEST


def extended(value, sides, width):
    for axis, dim in sides:
        size, length = (lax.axis_size(axis), value.shape[dim])
        up = [(i, (i + 1) % size) for i in range(size - 1)]
        down = [(j, i) for i, j in up]
        last = lax.slice_in_dim(value, length - width, length, axis=dim)
        first = lax.slice_in_dim(value, 0, width, axis=dim)
        before = lax.ppermute(last, axis, up)
        after = lax.ppermute(first, axis, down)
        value = jnp.concatenate([before, value, after], axis=dim)
    return value


def by_axis(value, axes):
    for axis in axes:
        value = lax.psum(value, axis)
    return value


def waves(count_first, count_second, length):
    product = (
        jnp.arange(count_first, dtype=jnp.int32)[:, None]
        * jnp.arange(count_second, dtype=jnp.int32)[None, :]
        % length
    )
    angle = product.astype(jnp.float32) * (2.0 * math.pi / length)
    return (jnp.cos(angle), jnp.sin(angle))


def contract(form, left, table):
    return jnp.einsum(form, left, table, precision=highest)


def forward_block(cosine, sine):
    return jnp.stack([jnp.stack([cosine, -sine], 1), jnp.stack([sine, cosine], 1)], 0)


def inverse_block(cosine, sine):
    return jnp.stack([jnp.stack([cosine, sine], 1), jnp.stack([-sine, cosine], 1)], 0)


def build_tables(columns, row_total):
    radix_cols = columns // 128
    radix_rows = row_total // 128
    first_cos, first_sin = waves(radix_cols, radix_cols, radix_cols)
    turn_cos, turn_sin = waves(radix_cols, 128, columns)
    inner_cos, inner_sin = waves(128, 128, 128)
    second_cos, second_sin = waves(radix_rows, radix_rows, radix_rows)
    spin_cos, spin_sin = waves(radix_rows, 128, row_total)
    first_start = jnp.stack([first_cos, -first_sin], 1)
    first_final = jnp.stack([first_cos, -first_sin], 0)
    return (
        first_start,
        first_final,
        turn_cos,
        turn_sin,
        forward_block(inner_cos, inner_sin),
        inverse_block(inner_cos, inner_sin),
        forward_block(second_cos, second_sin),
        inverse_block(second_cos, second_sin),
        spin_cos,
        spin_sin,
    )


def forward_fourier_map(volume, twiddle_tables):
    (
        first_start,
        first_final,
        turn_cos,
        turn_sin,
        inner_fwd,
        inner_inv,
        second_fwd,
        second_inv,
        spin_cos,
        spin_sin,
    ) = twiddle_tables
    batches, planes, row_count, columns = volume.shape
    groups = lax.axis_size(GY)
    per_group = 128 // row_count
    bins_here = columns // groups
    radix_cols = first_start.shape[0]
    radix_rows = second_fwd.shape[1]
    blocked = volume.reshape(batches, planes, row_count, radix_cols, 128)
    parts = contract("bzyan,adk->dbzykn", blocked, first_start)
    twisted = jnp.stack(
        [parts[0] * turn_cos + parts[1] * turn_sin, parts[1] * turn_cos - parts[0] * turn_sin], 0
    )
    across = contract("cbzykn,cndq->dbkqzy", twisted, inner_fwd)
    arrived = lax.all_to_all(
        across.reshape(2, batches, columns, planes * row_count),
        GY,
        split_axis=2,
        concat_axis=3,
        tiled=True,
    )
    arrived = arrived.reshape(2, batches, bins_here, radix_rows, per_group, planes, row_count)
    down = contract("cbpajzy,cadk->dbpkzjy", arrived, second_fwd)
    down = down.reshape(2, batches, bins_here, radix_rows, planes, 128)
    spin_real = spin_cos[:, None, :]
    spin_imaginary = spin_sin[:, None, :]
    spun = jnp.stack(
        [
            down[0] * spin_real + down[1] * spin_imaginary,
            down[1] * spin_real - down[0] * spin_imaginary,
        ],
        0,
    )
    return contract("cbpkzm,cmdq->dbpkzq", spun, inner_fwd)


def inverse_transform(spectrum, twiddle_tables):
    (
        first_start,
        first_final,
        turn_cos,
        turn_sin,
        inner_fwd,
        inner_inv,
        second_fwd,
        second_inv,
        spin_cos,
        spin_sin,
    ) = twiddle_tables
    unused, batches, bins_here, radix_rows, planes, width = spectrum.shape
    groups = lax.axis_size(GY)
    columns = bins_here * groups
    radix_cols = first_start.shape[0]
    row_count = radix_rows * 128 // groups
    per_group = 128 // row_count
    down = contract("cbpkzq,cqdm->dbpkzm", spectrum, inner_inv)
    spin_real = spin_cos[:, None, :]
    spin_imaginary = spin_sin[:, None, :]
    twist = jnp.stack(
        [
            down[0] * spin_real - down[1] * spin_imaginary,
            down[1] * spin_real + down[0] * spin_imaginary,
        ],
        0,
    )
    twist = twist.reshape(2, batches, bins_here, radix_rows, planes, per_group, row_count)
    rows_part = contract("cbpkzjy,ckda->dbpajzy", twist, second_inv)
    arrived = lax.all_to_all(
        rows_part.reshape(2, batches, bins_here, groups * planes * row_count),
        GY,
        split_axis=3,
        concat_axis=2,
        tiled=True,
    )
    arrived = arrived.reshape(2, batches, radix_cols, 128, planes, row_count)
    inner = contract("cbkqzy,cqdn->dbzykn", arrived, inner_inv)
    turned = jnp.stack(
        [inner[0] * turn_cos - inner[1] * turn_sin, inner[1] * turn_cos + inner[0] * turn_sin], 0
    )
    volume = contract("cbzykn,cka->bzyan", turned, first_final)
    return volume.reshape(batches, planes, row_count, columns) / float(columns * radix_rows * 128)


def filtered(volume, power_gain, twiddle_tables):
    spectrum = forward_fourier_map(volume[None], twiddle_tables)
    return inverse_transform(spectrum * power_gain, twiddle_tables)[0]


def extend(volume):
    grown = extended(volume, ((GY, 1), (GZ, 0)), 1)
    return jnp.pad(grown, ((0, 0), (0, 0), (1, 1)))


def stencil(grown, kernel, planes, row_count, columns):
    summed = jnp.zeros((planes, row_count, columns), jnp.float32)
    for shift_z in range(3):
        for shift_y in range(3):
            for shift_x in range(3):
                summed = (
                    summed
                    + kernel[shift_z, shift_y, shift_x]
                    * grown[
                        shift_z : shift_z + planes,
                        shift_y : shift_y + row_count,
                        shift_x : shift_x + columns,
                    ]
                )
    return summed


def correlate(values, grown):
    planes, row_count, columns = values.shape
    pieces = []
    for shift_z in range(3):
        for shift_y in range(3):
            for shift_x in range(3):
                pieces.append(
                    jnp.sum(
                        values
                        * grown[
                            shift_z : shift_z + planes,
                            shift_y : shift_y + row_count,
                            shift_x : shift_x + columns,
                        ]
                    )
                )
    return jnp.stack(pieces)


def regular(volume, kernel, flipped):
    planes, row_count, columns = volume.shape
    grown = extend(volume)
    mapped = stencil(grown, kernel, planes, row_count, columns)
    back = stencil(extend(mapped), flipped, planes, row_count, columns)
    return (back, grown, mapped)


def local(measured, point_spread, stencil_weights, upstream):
    planes, row_count, columns = measured.shape
    groups = lax.axis_size(GY)
    cells = planes * row_count * columns * groups * lax.axis_size(GZ)
    twiddle_tables = build_tables(columns, row_count * groups)
    flipped = stencil_weights[::-1, ::-1, ::-1]
    optical = forward_fourier_map(point_spread[None, None], twiddle_tables)
    optical_real = optical[0]
    optical_imaginary = optical[1]
    power_gain = optical_real * optical_real + optical_imaginary * optical_imaginary
    observed = forward_fourier_map(measured[None], twiddle_tables)
    adjoint_spectrum = jnp.stack(
        [
            observed[0] * optical_real + observed[1] * optical_imaginary,
            observed[1] * optical_real - observed[0] * optical_imaginary,
        ],
        0,
    )
    early_blur = None
    stacked = inverse_transform(
        jnp.concatenate([adjoint_spectrum, adjoint_spectrum * power_gain], axis=1), twiddle_tables
    )
    right_side = stacked[0]
    early_blur = stacked[1]
    directions = [right_side]
    residuals = [right_side]
    images = []
    norms = []
    curvatures = []
    step_sizes = []
    ratios = []
    grown_list = []
    mapped_list = []
    upward = []
    crossed = []
    norm_now = by_axis(jnp.sum(right_side * right_side), GY_GZ)
    for iteration in range(ITERS):
        direction = directions[iteration]
        back, grown, mapped = regular(direction, stencil_weights, flipped)
        if iteration == 0 and early_blur is not None:
            blurred = early_blur
        else:
            blurred = filtered(direction, power_gain, twiddle_tables)
        applied = blurred + back
        curvature, along = (
            by_axis(jnp.sum(direction * applied), GY_GZ),
            by_axis(jnp.sum(upstream * direction), GY_GZ),
        )
        upward.append(along)
        step_size = norm_now / curvature
        images.append(applied)
        norms.append(norm_now)
        curvatures.append(curvature)
        step_sizes.append(step_size)
        grown_list.append(grown)
        mapped_list.append(mapped)
        if iteration + 1 < ITERS:
            residual = residuals[iteration] - step_size * applied
            norm_next, cross = (
                by_axis(jnp.sum(residual * residual), GY_GZ),
                by_axis(jnp.sum(residual * applied), GY_GZ),
            )
            crossed.append(cross)
            ratio = norm_next / norm_now
            ratios.append(ratio)
            residuals.append(residual)
            directions.append(residual + ratio * direction)
            norm_now = norm_next
    grad_direction = None
    grad_residual = None
    grad_norm = 0.0
    stencil_terms = jnp.zeros((27,), jnp.float32)
    for iteration in reversed(range(ITERS)):
        direction = directions[iteration]
        applied = images[iteration]
        step_size = step_sizes[iteration]
        grad_step = upward[iteration]
        grad_new = step_size * upstream
        grad_norm_here = 0.0
        grad_residual_next = None
        if iteration + 1 < ITERS:
            grad_ratio, known_image = (
                by_axis(jnp.sum(grad_direction * direction), GY_GZ),
                by_axis(jnp.sum(grad_direction * applied), GY_GZ),
            )
            grad_norm = grad_norm + grad_ratio / norms[iteration]
            grad_image = known_image + 2.0 * grad_norm * crossed[iteration]
            grad_residual_next = grad_direction + 2.0 * grad_norm * residuals[iteration + 1]
            grad_step = grad_step - grad_image
            grad_new = grad_new + ratios[iteration] * grad_direction
            grad_norm_here = -grad_ratio * ratios[iteration] / norms[iteration]
        grad_norm_step = grad_norm_here + grad_step / curvatures[iteration]
        grad_curve = -grad_step * step_size / curvatures[iteration]
        grad_new = grad_new + 2.0 * grad_curve * applied
        mapped = mapped_list[iteration]
        grown = grown_list[iteration]
        if grad_residual_next is not None:
            back_other, grown_other, mapped_other = regular(
                grad_residual_next, stencil_weights, flipped
            )
            blurred_other = filtered(grad_residual_next, power_gain, twiddle_tables)
            grad_new = grad_new - step_size * (blurred_other + back_other)
            local_terms = correlate(
                2.0 * grad_curve * mapped - step_size * mapped_other, grown
            ) - step_size * correlate(mapped, grown_other)
        else:
            local_terms = correlate(2.0 * grad_curve * mapped, grown)
        stencil_terms = stencil_terms + local_terms
        grad_direction = grad_new
        grad_residual = grad_residual_next
        grad_norm = grad_norm_step
    stencil_terms = by_axis(stencil_terms, GY_GZ)
    grad_right = grad_direction + 2.0 * grad_norm * right_side
    grad_right = grad_right + grad_residual
    right_spectrum = forward_fourier_map(grad_right[None], twiddle_tables)
    product = jnp.stack(
        [
            right_spectrum[0] * optical_real - right_spectrum[1] * optical_imaginary,
            right_spectrum[1] * optical_real + right_spectrum[0] * optical_imaginary,
        ],
        0,
    )
    grad_measured = inverse_transform(product, twiddle_tables)[0]
    grad_stencil = stencil_terms.reshape(3, 3, 3) / math.sqrt(cells)
    return (grad_measured, grad_stencil)


def solution(mesh):
    finer = Mesh(mesh.devices.reshape(16, 2, 4, 4), ("gy_0", "gy_1", "gz_0", "gz_1"))
    return jax.shard_map(
        local,
        mesh=finer,
        in_specs=(P(GZ, GY, None), P(GY, None), P(), P(GZ, GY, None)),
        out_specs=(P(GZ, GY, None), P()),
        check_vma=False,
    )
```

profile of v0, /device:TPU:2, one launch (start us, length us, event | category | flops | bytes accessed | tf_op | source)
XLA Modules:
  0.0 902.2 jit_solution(1123461139081819542)
XLA Ops:
  6.9 15.5 %all-to-all-start.1 = ((f32[32,1,2048]{2,1,0:T(1,128)}), f32[32,1,2048]{2,1,0:T(1,128)S(1)}, u32[]{:S(2)}, u32[]{:S(2)}) async-start(f32[32,1,2048]{2,1,0:T(1,128)} %reshape.1333), calls=%async_computation.1 | async-start | bytes 524288 | tf_op jit(solution)/shard_map/all_to_all | solution.py:105
  25.4 19.8 %all-to-all-done.1 = f32[32,1,2048]{2,1,0:T(1,128)S(1)} async-done(((f32[32,1,2048]{2,1,0:T(1,128)}), f32[32,1,2048]{2,1,0:T(1,128)S(1)}, u32[]{:S(2)}, u32[]{:S(2)}) %all-to-all-start.1) | async-done | bytes 262176 | tf_op jit(solution)/shard_map/all_to_all | solution.py:105
  45.2 4.0 all-to-all-start
  55.6 16.3 %all-to-all-done = f32[32,1,2048]{2,1,0:T(1,128)S(1)} async-done(((f32[32,1,2048]{2,1,0:T(1,128)}), f32[32,1,2048]{2,1,0:T(1,128)S(1)}, u32[]{:S(2)}, u32[]{:S(2)}) %all-to-all-start) | async-done | bytes 262176 | tf_op jit(solution)/shard_map/all_to_all | solution.py:105
  82.7 3.3 fusion.3
  92.0 3.9 all-to-all-start.2
  95.9 33.9 %all-to-all-done.2 = f32[32,1,4096]{2,1,0:T(1,128)S(1)} async-done(((f32[32,1,4096]{2,1,0:T(1,128)}), f32[32,1,4096]{2,1,0:T(1,128)S(1)}, u32[]{:S(2)}, u32[]{:S(2)}) %all-to-all-start.2) | async-done | bytes 524320 | tf_op jit(solution)/shard_map/all_to_all | solution.py:158
  149.2 3.6 collective-permute-start.2
  158.0 17.3 %multiply_add_fusion.20 = f32[1,32,1024]{2,1,0:T(8,128)S(1)} fusion(f32[1,32,1024]{2,1,0:T(8,128)S(1)} %squeeze.82, f32[3,34,1026]{2,1,0:T(8,128)S(1)} %select_maximum_fusion.20, f32[1,34,1024]{2,1,0:T(8,128)S(1)} %collective-permute-done.3, f32[1,34,1024]{2,1,0:T(8,128)S(1)} %collective-permute-done.2, f32[1,1,1024]{2,1,0:T(1,128)S(1)} %collective-permute-done, ...), kind=kLoop, calls=%fused_computation.485 | loop fusion | flops 1802240 | bytes 3416172 | tf_op jit(solution)/shard_map/add | solution.py:190
  182.5 3.9 collective-permute-start.6
  191.5 18.0 %multiply_reduce_fusion.88 = (f32[]{:T(128)}, f32[]{:T(128)}, f32[1,32,1024]{2,1,0:T(8,128)S(1)}) fusion(f32[1,32,1024]{2,1,0:T(8,128)S(1)} %squeeze.82, f32[1,32,1024]{2,1,0:T(8,128)S(1)} %squeeze.83, f32[3,34,1026]{2,1,0:T(8,128)S(1)} %select_maximum_fusion.16, f32[]{:T(128)} %bitcast.113, f32[1,34,1024]{2,1,0:T(8,128)S(1)} %collective-permute-done.7, ...), kind=kLoop, calls=%fused_computation.484 | loop fusion | flops 1966078 | bytes 3678324 | tf_op jit(solution)/shard_map/reduce_sum | solution.py:273
  209.5 29.5 %all-reduce.8 = (f32[]{:T(128)}, f32[]{:T(128)}) all-reduce(f32[]{:T(128)} %get-tuple-element.109, f32[]{:T(128)} %get-tuple-element.108), channel_id=1, replica_groups=mesh['gy_0'=16,'gy_1'=2,'gz_0'=4,'gz_1'=4] {'gy_0'}, use_global_device_ids=true, to_apply=%region_1.2 | all-reduce | flops 2 | bytes 16 | tf_op jit(solution)/shard_map/psum | solution.py:30
  242.1 16.5 %all-reduce.14 = (f32[]{:T(128)}, f32[]{:T(128)}) all-reduce(f32[]{:T(128)} %get-tuple-element.140, f32[]{:T(128)} %get-tuple-element.141), channel_id=1, replica_groups=mesh['gy_0'=16,'gy_1'=2,'gz_0'=4,'gz_1'=4] {'gz_0'}, use_global_device_ids=true, to_apply=%region_3.4 | all-reduce | flops 2 | bytes 16 | tf_op jit(solution)/shard_map/psum | solution.py:30
  258.6 10.5 %all-reduce.11 = (f32[]{:T(128)}, f32[]{:T(128)}) all-reduce(f32[]{:T(128)} %get-tuple-element.132, f32[]{:T(128)} %get-tuple-element.133), channel_id=1, replica_groups=mesh['gy_0'=16,'gy_1'=2,'gz_0'=4,'gz_1'=4] {'gz_1'}, use_global_device_ids=true, to_apply=%region_4.5 | all-reduce | flops 2 | bytes 16 | tf_op jit(solution)/shard_map/psum | solution.py:30
  271.2 27.8 %psum.288 = f32[]{:T(128)} all-reduce(f32[]{:T(128)} %get-tuple-element.83), channel_id=1, replica_groups=mesh['gy_0'=16,'gy_1'=2,'gz_0'=4,'gz_1'=4] {'gy_0'}, use_global_device_ids=true, to_apply=%region_11.12 | all-reduce | flops 1 | bytes 8 | tf_op jit(solution)/shard_map/psum | solution.py:30
  302.1 8.3 psum.290
  310.4 8.5 psum.291
  325.2 8.0 all-to-all-start.3
  339.0 3.9 collective-permute-start.11
  344.9 11.2 %all-to-all-done.3 = f32[32,1,2048]{2,1,0:T(1,128)S(1)} async-done(((f32[32,1,2048]{2,1,0:T(1,128)}), f32[32,1,2048]{2,1,0:T(1,128)S(1)}, u32[]{:S(2)}, u32[]{:S(2)}) %all-to-all-start.3) | async-done | bytes 262176 | tf_op jit(solution)/shard_map/all_to_all | solution.py:105
  372.0 8.7 all-to-all-start.4
  381.0 17.3 %multiply_add_fusion.14 = f32[1,32,1024]{2,1,0:T(8,128)S(1)} fusion(f32[1,32,1024]{2,1,0:T(8,128)S(1)} %multiply_add_fusion.19, f32[3,34,1026]{2,1,0:T(8,128)S(1)} %select_maximum_fusion.12, f32[1,34,1024]{2,1,0:T(8,128)S(1)} %collective-permute-done.11, f32[1,34,1024]{2,1,0:T(8,128)S(1)} %collective-permute-done.10, ...), kind=kLoop, calls=%fused_computation.472 | loop fusion | flops 1802240 | bytes 3416172 | tf_op jit(solution)/shard_map/add | solution.py:190
  403.5 3.9 collective-permute-start.15
  412.1 4.1 collective-permute-done.14
  432.0 19.8 %multiply_reduce_fusion.86 = (f32[]{:T(128)}, f32[]{:T(128)}, f32[1,32,1024]{2,1,0:T(8,128)}) fusion(f32[1,32,1024]{2,1,0:T(8,128)S(1)} %multiply_add_fusion.19, f32[1,32,1024]{2,1,0:T(8,128)S(1)} %copy-done.11, f32[1,32,1024]{2,1,0:T(8,128)} %div.78, f32[3,34,1026]{2,1,0:T(8,128)S(1)} %select_maximum_fusion.8, f32[]{:T(128)} %bitcast.113, ...), kind=kLoop, calls=%fused_computation.471 | loop fusion | flops 1966078 | bytes 3809396 | tf_op jit(solution)/shard_map/reduce_sum | solution.py:273
  451.8 32.6 %all-reduce.7 = (f32[]{:T(128)}, f32[]{:T(128)}) all-reduce(f32[]{:T(128)} %get-tuple-element.107, f32[]{:T(128)} %get-tuple-element.106), channel_id=1, replica_groups=mesh['gy_0'=16,'gy_1'=2,'gz_0'=4,'gz_1'=4] {'gy_0'}, use_global_device_ids=true, to_apply=%region_21.22 | all-reduce | flops 2 | bytes 16 | tf_op jit(solution)/shard_map/psum | solution.py:30
  487.6 10.8 %all-reduce.13 = (f32[]{:T(128)}, f32[]{:T(128)}) all-reduce(f32[]{:T(128)} %get-tuple-element.138, f32[]{:T(128)} %get-tuple-element.139), channel_id=1, replica_groups=mesh['gy_0'=16,'gy_1'=2,'gz_0'=4,'gz_1'=4] {'gz_0'}, use_global_device_ids=true, to_apply=%region_23.24 | all-reduce | flops 2 | bytes 16 | tf_op jit(solution)/shard_map/psum | solution.py:30
  498.4 12.3 %all-reduce.10 = (f32[]{:T(128)}, f32[]{:T(128)}) all-reduce(f32[]{:T(128)} %get-tuple-element.130, f32[]{:T(128)} %get-tuple-element.131), channel_id=1, replica_groups=mesh['gy_0'=16,'gy_1'=2,'gz_0'=4,'gz_1'=4] {'gz_1'}, use_global_device_ids=true, to_apply=%region_24.25 | all-reduce | flops 2 | bytes 16 | tf_op jit(solution)/shard_map/psum | solution.py:30
  516.5 30.6 %all-reduce.6 = (f32[]{:T(128)}, f32[]{:T(128)}, f32[]{:T(128)}, f32[]{:T(128)}) all-reduce(f32[]{:T(128)} %get-tuple-element.105, f32[]{:T(128)} %get-tuple-element.103, f32[]{:T(128)} %get-tuple-element.104, f32[]{:T(128)} %get-tuple-element.82), channel_id=1, replica_groups=mesh['gy_0'=16,'gy_1'=2,'gz_0'=4,'gz_1'=4] {'gy_0'}, use_global_device_ids=true, to_apply=%region_36.37 | all-reduce | flops 4 | bytes 32 | tf_op jit(solution)/shard_map/psum | solution.py:30
  550.3 9.3 %all-reduce.12 = (f32[]{:T(128)}, f32[]{:T(128)}, f32[]{:T(128)}, f32[]{:T(128)}) all-reduce(f32[]{:T(128)} %get-tuple-element.134, f32[]{:T(128)} %get-tuple-element.135, f32[]{:T(128)} %get-tuple-element.136, f32[]{:T(128)} %get-tuple-element.137), channel_id=1, replica_groups=mesh['gy_0'=16,'gy_1'=2,'gz_0'=4,'gz_1'=4] {'gz_0'}, use_global_device_ids=true, to_apply=%region_38.39 | all-reduce | flops 4 | bytes 32 | tf_op jit(solution)/shard_map/psum | solution.py:30
  559.6 8.4 all-reduce.9
  574.6 7.9 all-to-all-start.5
  590.3 3.9 collective-permute-start.19
  596.6 8.9 all-to-all-done.5
  631.1 9.1 %all-to-all-start.6 = ((f32[32,1,2048]{2,1,0:T(1,128)}), f32[32,1,2048]{2,1,0:T(1,128)}, u32[]{:S(2)}, u32[]{:S(2)}) async-start(f32[32,1,2048]{2,1,0:T(1,128)} %reshape.1343), calls=%async_computation.6 | async-start | bytes 524288 | tf_op jit(solution)/shard_map/all_to_all | solution.py:158
  640.5 18.8 %multiply_reduce_fusion.28 = (f32[]{:T(128)}, f32[]{:T(128)}, f32[]{:T(128)}, f32[]{:T(128)}, f32[]{:T(128)}, /*index=5*/f32[]{:T(128)}, f32[]{:T(128)}, f32[]{:...) fusion(f32[1,34,1024]{2,1,0:T(8,128)S(1)} %collective-permute-done.3, ...), kind=kLoop, calls=%fused_computation.391 | loop fusion | flops 2555895 | bytes 4604056 | tf_op jit(solution)/shard_map/reduce_sum | solution.py:208
  664.5 3.9 collective-permute-start.23
  673.8 3.6 collective-permute-done.22
  693.5 18.9 %fusion.91 = f32[4,8,8,128]{3,1,2,0:T(8,128)S(1)} fusion(f32[1,32,1024]{2,1,0:T(8,128)S(1)} %multiply_add_fusion.12, f32[1,32,1024]{2,1,0:T(8,128)} %div.87, f32[3,34,1026]{2,1,0:T(8,128)S(1)} %select_maximum_fusion, f32[1,34,1024]{2,1,0:T(8,128)} %copy-done.15, f32[1,1,1024]{2,1,0:T(1,128)} %copy-done.27, f32[1,32,1024]{2,1,0:T(8,128)} %copy-done.10, ...), kind=kLoop, calls=%fused_computation.194 | loop fusion | flops 2162688 | bytes 4202620
  717.8 13.9 %all-to-all-start.7 = ((f32[32,1,2048]{2,1,0:T(1,128)}), f32[32,1,2048]{2,1,0:T(1,128)S(1)}, u32[]{:S(2)}, u32[]{:S(2)}) async-start(f32[32,1,2048]{2,1,0:T(1,128)} %reshape.1345), calls=%async_computation.7 | async-start | bytes 524288 | tf_op jit(solution)/shard_map/all_to_all | solution.py:105
  732.9 21.6 %all-to-all-done.7 = f32[32,1,2048]{2,1,0:T(1,128)S(1)} async-done(((f32[32,1,2048]{2,1,0:T(1,128)}), f32[32,1,2048]{2,1,0:T(1,128)S(1)}, u32[]{:S(2)}, u32[]{:S(2)}) %all-to-all-start.7) | async-done | bytes 262176 | tf_op jit(solution)/shard_map/all_to_all | solution.py:105
  783.4 3.9 all-to-all-start.8
  788.1 16.7 %stack.528 = f32[27]{0:T(128)S(1)} concatenate(f32[1]{0:T(128)} %bitcast.305, f32[1]{0:T(128)} %bitcast.306, f32[1]{0:T(128)} %bitcast.307, f32[1]{0:T(128)} %bitcast.308, f32[1]{0:T(128)} %bitcast.309, f32[1]{0:T(128)} %bitcast.310, f32[1]{0:T(128)} %bitcast.311, f32[1]{0:T(128)} %bitcast.312, f32[1]{0:T(128)} %bitcast.313, f32[1]{0:T(128)} %bitcast.314, f32[1]{0:T(128)} %bitcast.315, ...), dimensions={0} | concatenate | bytes 216 | tf_op jit(solution)/shard_map/stack | solution.py:217
  806.0 17.0 %stack.556 = f32[27]{0:T(128)S(1)} concatenate(f32[1]{0:T(128)} %bitcast.332, f32[1]{0:T(128)} %bitcast.333, f32[1]{0:T(128)} %bitcast.334, f32[1]{0:T(128)} %bitcast.335, f32[1]{0:T(128)} %bitcast.336, f32[1]{0:T(128)} %bitcast.337, f32[1]{0:T(128)} %bitcast.338, f32[1]{0:T(128)} %bitcast.339, f32[1]{0:T(128)} %bitcast.340, f32[1]{0:T(128)} %bitcast.341, f32[1]{0:T(128)} %bitcast.342, ...), dimensions={0} | concatenate | bytes 216 | tf_op jit(solution)/shard_map/stack | solution.py:217
  825.0 17.2 %stack.584 = f32[27]{0:T(128)S(1)} concatenate(f32[1]{0:T(128)} %bitcast.359, f32[1]{0:T(128)} %bitcast.360, f32[1]{0:T(128)} %bitcast.361, f32[1]{0:T(128)} %bitcast.362, f32[1]{0:T(128)} %bitcast.363, f32[1]{0:T(128)} %bitcast.364, f32[1]{0:T(128)} %bitcast.365, f32[1]{0:T(128)} %bitcast.366, f32[1]{0:T(128)} %bitcast.367, f32[1]{0:T(128)} %bitcast.368, f32[1]{0:T(128)} %bitcast.369, ...), dimensions={0} | concatenate | bytes 216 | tf_op jit(solution)/shard_map/stack | solution.py:217
  842.2 30.6 %psum.316 = f32[27]{0:T(128)S(1)} all-reduce(f32[27]{0:T(128)S(1)} %subtract_add_fusion), channel_id=1, replica_groups=mesh['gy_0'=16,'gy_1'=2,'gz_0'=4,'gz_1'=4] {'gy_0'}, use_global_device_ids=true, to_apply=%region_126.127 | all-reduce | flops 27 | bytes 216 | tf_op jit(solution)/shard_map/psum | solution.py:30
  875.3 9.3 %psum.318 = f32[27]{0:T(128)S(1)} all-reduce(f32[27]{0:T(128)S(1)} %psum.317), channel_id=1, replica_groups=mesh['gy_0'=16,'gy_1'=2,'gz_0'=4,'gz_1'=4] {'gz_0'}, use_global_device_ids=true, to_apply=%region_128.129 | all-reduce | flops 27 | bytes 216 | tf_op jit(solution)/shard_map/psum | solution.py:30
  884.6 12.1 %psum.319 = f32[27]{0:T(128)S(1)} all-reduce(f32[27]{0:T(128)S(1)} %psum.318), channel_id=1, replica_groups=mesh['gy_0'=16,'gy_1'=2,'gz_0'=4,'gz_1'=4] {'gz_1'}, use_global_device_ids=true, to_apply=%region_129.130 | all-reduce | flops 27 | bytes 216 | tf_op jit(solution)/shard_map/psum | solution.py:30
  (316 shorter events, 247.8 us)
Async XLA Ops:
  6.9 38.2 %all-to-all-start.1 = ((f32[32,1,2048]{2,1,0:T(1,128)}), f32[32,1,2048]{2,1,0:T(1,128)S(1)}, u32[]{:S(2)}, u32[]{:S(2)}) async-start(f32[32,1,2048]{2,1,0:T(1,128)} %reshape.1333), calls=%async_computation.1 | async-start | bytes 524288 | tf_op jit(solution)/shard_map/all_to_all | solution.py:105
  45.2 26.7 %all-to-all-start = ((f32[32,1,2048]{2,1,0:T(1,128)}), f32[32,1,2048]{2,1,0:T(1,128)S(1)}, u32[]{:S(2)}, u32[]{:S(2)}) async-start(f32[32,1,2048]{2,1,0:T(1,128)} %reshape.1331), calls=%async_computation | async-start | bytes 524288 | tf_op jit(solution)/shard_map/all_to_all | solution.py:105
  77.7 286.8 %copy-start.12 = (f32[32,8,128]{2,0,1:T(8,128)}, f32[32,8,128]{2,0,1:T(8,128)S(1)}, u32[]{:S(2)}) copy-start(f32[32,8,128]{2,0,1:T(8,128)S(1)} %get-tuple-element.202) | copy-start | bytes 393220
  92.0 37.9 %all-to-all-start.2 = ((f32[32,1,4096]{2,1,0:T(1,128)}), f32[32,1,4096]{2,1,0:T(1,128)S(1)}, u32[]{:S(2)}, u32[]{:S(2)}) async-start(f32[32,1,4096]{2,1,0:T(1,128)} %reshape.1335), calls=%async_computation.2 | async-start | bytes 1048576 | tf_op jit(solution)/shard_map/all_to_all | solution.py:158
  141.6 4.3 collective-permute-start.1
  142.9 3.8 collective-permute-start
  145.9 29.4 %copy-start.19 = (f32[1,1,1024]{2,1,0:T(1,128)}, f32[1,1,1024]{2,1,0:T(1,128)S(1)}, u32[]{:S(2)}) copy-start(f32[1,1,1024]{2,1,0:T(1,128)S(1)} %collective-permute-done.1) | copy-start | bytes 12292
  146.7 28.6 %copy-start.21 = (f32[1,1,1024]{2,1,0:T(1,128)}, f32[1,1,1024]{2,1,0:T(1,128)S(1)}, u32[]{:S(2)}) copy-start(f32[1,1,1024]{2,1,0:T(1,128)S(1)} %collective-permute-done) | copy-start | bytes 12292
  146.8 8.9 collective-permute-start.3
  149.2 8.6 collective-permute-start.2
  175.4 4.3 collective-permute-start.5
  176.7 3.8 collective-permute-start.4
  180.6 8.7 collective-permute-start.7
  182.5 8.7 collective-permute-start.6
  191.5 79.0 %copy-start.11 = (f32[1,32,1024]{2,1,0:T(8,128)S(1)}, f32[1,32,1024]{2,1,0:T(8,128)}, u32[]{:S(2)}) copy-start(f32[1,32,1024]{2,1,0:T(8,128)} %param.7) | copy-start | bytes 393220
  209.5 359.8 %copy-start.4 = (f32[1,32,1024]{2,1,0:T(8,128)}, f32[1,32,1024]{2,1,0:T(8,128)S(1)}, u32[]{:S(2)}) copy-start(f32[1,32,1024]{2,1,0:T(8,128)S(1)} %get-tuple-element.146) | copy-start | bytes 393220
  325.2 30.9 %all-to-all-start.3 = ((f32[32,1,2048]{2,1,0:T(1,128)}), f32[32,1,2048]{2,1,0:T(1,128)S(1)}, u32[]{:S(2)}, u32[]{:S(2)}) async-start(f32[32,1,2048]{2,1,0:T(1,128)} %reshape.1337), calls=%async_computation.3 | async-start | bytes 524288 | tf_op jit(solution)/shard_map/all_to_all | solution.py:105
  333.2 4.3 collective-permute-start.9
  334.5 3.8 collective-permute-start.8
  339.0 41.7 %collective-permute-start.11 = (f32[1,34,1024]{2,1,0:T(8,128)}, f32[1,34,1024]{2,1,0:T(8,128)S(1)}, u32[]{:S(2)}, u32[]{:S(2)}) collective-permute-start(f32[1,34,1024]{2,1,0:T(8,128)} %pad_maximum_fusion.3), channel_id=1, source_target_pairs={{1,0},{2,1},{3,2},{4,3},{5,4},{6,5},{7,6},{8,7},{9,8},{10,9},{11,1... | collective-permute-start | bytes 417800 | tf_op jit(solution)/shard_map/ppermute | solution.py:23
  343.0 37.8 %collective-permute-start.10 = (f32[1,34,1024]{2,1,0:T(8,128)}, f32[1,34,1024]{2,1,0:T(8,128)S(1)}, u32[]{:S(2)}, u32[]{:S(2)}) collective-permute-start(f32[1,34,1024]{2,1,0:T(8,128)} %pad_maximum_fusion.3), channel_id=1, source_target_pairs={{0,1},{1,2},{2,3},{3,4},{4,5},{5,6},{6,7},{7,8},{8,9},{9,10},{10,1... | collective-permute-start | bytes 417800 | tf_op jit(solution)/shard_map/ppermute | solution.py:22
  372.0 45.2 %all-to-all-start.4 = ((f32[32,1,2048]{2,1,0:T(1,128)}), f32[32,1,2048]{2,1,0:T(1,128)}, u32[]{:S(2)}, u32[]{:S(2)}) async-start(f32[32,1,2048]{2,1,0:T(1,128)} %reshape.1339), calls=%async_computation.4 | async-start | bytes 524288 | tf_op jit(solution)/shard_map/all_to_all | solution.py:158
  380.7 17.6 %copy-start = (f32[1,34,1024]{2,1,0:T(8,128)}, f32[1,34,1024]{2,1,0:T(8,128)S(1)}, u32[]{:S(2)}) copy-start(f32[1,34,1024]{2,1,0:T(8,128)S(1)} %collective-permute-done.10) | copy-start | bytes 417796
  398.3 33.7 %copy-start.2 = (f32[1,32,1024]{2,1,0:T(8,128)}, f32[1,32,1024]{2,1,0:T(8,128)S(1)}, u32[]{:S(2)}) copy-start(f32[1,32,1024]{2,1,0:T(8,128)S(1)} %multiply_add_fusion.14) | copy-start | bytes 393220
  398.3 4.3 collective-permute-start.13
  399.6 3.8 collective-permute-start.12
  403.5 8.7 collective-permute-start.15
  407.4 8.8 collective-permute-start.14
  516.5 55.1 %copy-start.16 = (f32[1,32,1024]{2,1,0:T(8,128)}, f32[1,32,1024]{2,1,0:T(8,128)S(1)}, u32[]{:S(2)}) copy-start(f32[1,32,1024]{2,1,0:T(8,128)S(1)} %get-tuple-element.144) | copy-start | bytes 393220
  574.6 30.8 %all-to-all-start.5 = ((f32[32,1,2048]{2,1,0:T(1,128)}), f32[32,1,2048]{2,1,0:T(1,128)S(1)}, u32[]{:S(2)}, u32[]{:S(2)}) async-start(f32[32,1,2048]{2,1,0:T(1,128)} %reshape.1341), calls=%async_computation.5 | async-start | bytes 524288 | tf_op jit(solution)/shard_map/all_to_all | solution.py:105
  582.6 7.0 collective-permute-start.17
  583.9 5.7 collective-permute-start.16
  589.6 50.9 %copy-start.23 = (f32[1,1,1024]{2,1,0:T(1,128)}, f32[1,1,1024]{2,1,0:T(1,128)S(1)}, u32[]{:S(2)}) copy-start(f32[1,1,1024]{2,1,0:T(1,128)S(1)} %collective-permute-done.17) | copy-start | bytes 12292
  589.6 50.8 %copy-start.25 = (f32[1,1,1024]{2,1,0:T(1,128)}, f32[1,1,1024]{2,1,0:T(1,128)S(1)}, u32[]{:S(2)}) copy-start(f32[1,1,1024]{2,1,0:T(1,128)S(1)} %collective-permute-done.16) | copy-start | bytes 12292
  590.3 49.9 %collective-permute-start.19 = (f32[1,34,1024]{2,1,0:T(8,128)}, f32[1,34,1024]{2,1,0:T(8,128)S(1)}, u32[]{:S(2)}, u32[]{:S(2)}) collective-permute-start(f32[1,34,1024]{2,1,0:T(8,128)} %pad_maximum_fusion.5), channel_id=1, source_target_pairs={{1,0},{2,1},{3,2},{4,3},{5,4},{6,5},{7,6},{8,7},{9,8},{10,9},{11,1... | collective-permute-start | bytes 417800 | tf_op jit(solution)/shard_map/ppermute | solution.py:23
  594.2 46.0 %collective-permute-start.18 = (f32[1,34,1024]{2,1,0:T(8,128)}, f32[1,34,1024]{2,1,0:T(8,128)S(1)}, u32[]{:S(2)}, u32[]{:S(2)}) collective-permute-start(f32[1,34,1024]{2,1,0:T(8,128)} %pad_maximum_fusion.5), channel_id=1, source_target_pairs={{0,1},{1,2},{2,3},{3,4},{4,5},{5,6},{6,7},{7,8},{8,9},{9,10},{10,1... | collective-permute-start | bytes 417800 | tf_op jit(solution)/shard_map/ppermute | solution.py:22
  625.7 14.8 %copy-start.22 = (f32[1,1,1024]{2,1,0:T(1,128)S(1)}, f32[1,1,1024]{2,1,0:T(1,128)}, u32[]{:S(2)}) copy-start(f32[1,1,1024]{2,1,0:T(1,128)} %copy-done.21) | copy-start | bytes 12292
  631.1 47.6 %all-to-all-start.6 = ((f32[32,1,2048]{2,1,0:T(1,128)}), f32[32,1,2048]{2,1,0:T(1,128)}, u32[]{:S(2)}, u32[]{:S(2)}) async-start(f32[32,1,2048]{2,1,0:T(1,128)} %reshape.1343), calls=%async_computation.6 | async-start | bytes 524288 | tf_op jit(solution)/shard_map/all_to_all | solution.py:158
  659.3 4.3 collective-permute-start.21
  660.6 3.8 collective-permute-start.20
  664.5 8.7 collective-permute-start.23
  668.4 9.0 collective-permute-start.22
  712.9 18.8 %copy-start.3 = (f32[1,32,1024]{2,1,0:T(8,128)S(1)}, f32[1,32,1024]{2,1,0:T(8,128)}, u32[]{:S(2)}) copy-start(f32[1,32,1024]{2,1,0:T(8,128)} %copy-done.2) | copy-start | bytes 393220
  717.8 36.7 %all-to-all-start.7 = ((f32[32,1,2048]{2,1,0:T(1,128)}), f32[32,1,2048]{2,1,0:T(1,128)S(1)}, u32[]{:S(2)}, u32[]{:S(2)}) async-start(f32[32,1,2048]{2,1,0:T(1,128)} %reshape.1345), calls=%async_computation.7 | async-start | bytes 524288 | tf_op jit(solution)/shard_map/all_to_all | solution.py:105
  780.4 24.4 %copy-start.17 = (f32[1,32,1024]{2,1,0:T(8,128)S(1)}, f32[1,32,1024]{2,1,0:T(8,128)}, u32[]{:S(2)}) copy-start(f32[1,32,1024]{2,1,0:T(8,128)} %get-tuple-element.142) | copy-start | bytes 393220
  783.4 113.9 %all-to-all-start.8 = ((f32[32,1,2048]{2,1,0:T(1,128)}), f32[32,1,2048]{2,1,0:T(1,128)S(1)}, u32[]{:S(2)}, u32[]{:S(2)}) async-start(f32[32,1,2048]{2,1,0:T(1,128)} %reshape.1347), calls=%async_computation.8 | async-start | bytes 524288 | tf_op jit(solution)/shard_map/all_to_all | solution.py:158
  787.3 35.7 %copy-start.24 = (f32[1,1,1024]{2,1,0:T(1,128)S(1)}, f32[1,1,1024]{2,1,0:T(1,128)}, u32[]{:S(2)}) copy-start(f32[1,1,1024]{2,1,0:T(1,128)} %copy-done.23) | copy-start | bytes 12292
  787.3 35.7 %copy-start.26 = (f32[1,1,1024]{2,1,0:T(1,128)S(1)}, f32[1,1,1024]{2,1,0:T(1,128)}, u32[]{:S(2)}) copy-start(f32[1,1,1024]{2,1,0:T(1,128)} %copy-done.25) | copy-start | bytes 12292
  (15 other events, 101.0 us)
where the time goes:
time: 912 us; the launch traced here: 902 us
  blocking collectives  272 us (30%)
  local copies, waits for them, and re-layouts  164 us (18%)
  other arithmetic  144 us (16%)
  starting transfers between devices  137 us (15%)
  waiting for transfers between devices  135 us (15%)
  matrix products  34.8 us (4%)
  between operations  15.3 us (2%)
    psum x20, blocking collectives, by_axis(): value = lax.psum(value, axis)  272 us
    all_to_all x5, waiting for transfers between devices, forward_fourier_map(): lax.all_to_all(across.reshape(2, batches, columns, planes * row_count), G...  77.7 us
    another operation x3, local copies, waits for them, and re-layouts, correlate(): return jnp.stack(pieces)  50.9 us
    all_to_all x5, starting transfers between devices, forward_fourier_map(): lax.all_to_all(across.reshape(2, batches, columns, planes * row_count), G...  49.4 us
    unnamed x83, local copies, waits for them, and re-layouts  42.1 us
    reduce_sum x2, other arithmetic, local(): jnp.sum(direction * applied)  37.8 us
    dot_general x36, matrix products, contract(): return jnp.einsum(form, left, table, precision=highest)  34.8 us
    add x2, other arithmetic, stencil(): summed + kernel[shift_z, shift_y, shift_x] * grown[shift_z:shift_z + plan...  34.6 us
  transfers between devices with their start and end apart: 33, of which 19 were waited for; matrix products, arithmetic and copies ran while one was open for 16% of the time, Pallas kernels for 0%

commit v1 on v0

--- a/solution.py
+++ b/solution.py
@@ -27,7 +27,7 @@
 
 def by_axis(value, axes):
     for axis in axes:
-        value = lax.psum(value, axis)
+        value = jnp.sum(lax.all_gather(value, axis), axis=0)
     return value
 
 

time: 912 us -> 974 us (1.068)
  local copies, waits for them, and re-layouts: 164 us -> 220 us
  other arithmetic: 144 us -> 167 us
  blocking collectives: 272 us -> 260 us
    psum x20 -> x0, blocking collectives: 272 us -> none  [by_axis(): value = lax.psum(value, axis)]
    unnamed x0 -> x19, blocking collectives: none -> 230 us
    unnamed x83 -> x161, local copies, waits for them, and re-layouts: 42.1 us -> 97.7 us
    all_gather x0 -> x1, blocking collectives: none -> 29.6 us  [by_axis(): value = jnp.sum(lax.all_gather(value, axis), axis=0)]
    reduce_sum x0 -> x40, other arithmetic: none -> 22.1 us  [by_axis(): value = jnp.sum(lax.all_gather(value, axis), axis=0)]
where the time goes in v1:
time: 974 us; the launch traced here: 963 us
  blocking collectives  260 us (27%)
  local copies, waits for them, and re-layouts  220 us (23%)
  other arithmetic  167 us (17%)
  starting transfers between devices  137 us (14%)
  waiting for transfers between devices  129 us (13%)
  matrix products  34.8 us (4%)
  between operations  16.8 us (2%)
    unnamed x19, blocking collectives  230 us
    unnamed x161, local copies, waits for them, and re-layouts  97.7 us
    all_to_all x5, waiting for transfers between devices, forward_fourier_map(): lax.all_to_all(across.reshape(2, batches, columns, planes * row_count), G...  74.2 us
    another operation x3, local copies, waits for them, and re-layouts, correlate(): return jnp.stack(pieces)  51.1 us
    all_to_all x5, starting transfers between devices, forward_fourier_map(): lax.all_to_all(across.reshape(2, batches, columns, planes * row_count), G...  49.4 us
    reduce_sum x2, other arithmetic, local(): jnp.sum(direction * applied)  38 us
    add x2, other arithmetic, stencil(): summed + kernel[shift_z, shift_y, shift_x] * grown[shift_z:shift_z + plan...  34.8 us
    dot_general x36, matrix products, contract(): return jnp.einsum(form, left, table, precision=highest)  34.8 us
  transfers between devices with their start and end apart: 33, of which 19 were waited for; matrix products, arithmetic and copies ran while one was open for 16% of the time, Pallas kernels for 0%

profile of v1, /device:TPU:2, one launch (start us, length us, event | category | flops | bytes accessed | tf_op | source)
XLA Modules:
  0.0 963.2 jit_solution(11499157647593629578)
XLA Ops:
  6.9 15.5 %all-to-all-start.1 = ((f32[32,1,2048]{2,1,0:T(1,128)}), f32[32,1,2048]{2,1,0:T(1,128)S(1)}, u32[]{:S(2)}, u32[]{:S(2)}) async-start(f32[32,1,2048]{2,1,0:T(1,128)} %reshape.2676), calls=%async_computation.1 | async-start | bytes 524288 | tf_op jit(solution)/shard_map/all_to_all | solution.py:105
  25.4 19.8 %all-to-all-done.1 = f32[32,1,2048]{2,1,0:T(1,128)S(1)} async-done(((f32[32,1,2048]{2,1,0:T(1,128)}), f32[32,1,2048]{2,1,0:T(1,128)S(1)}, u32[]{:S(2)}, u32[]{:S(2)}) %all-to-all-start.1) | async-done | bytes 262176 | tf_op jit(solution)/shard_map/all_to_all | solution.py:105
  45.2 4.1 all-to-all-start
  55.6 16.2 %all-to-all-done = f32[32,1,2048]{2,1,0:T(1,128)S(1)} async-done(((f32[32,1,2048]{2,1,0:T(1,128)}), f32[32,1,2048]{2,1,0:T(1,128)S(1)}, u32[]{:S(2)}, u32[]{:S(2)}) %all-to-all-start) | async-done | bytes 262176 | tf_op jit(solution)/shard_map/all_to_all | solution.py:105
  82.7 3.3 fusion.3
  92.0 3.9 all-to-all-start.2
  95.9 33.9 %all-to-all-done.2 = f32[32,1,4096]{2,1,0:T(1,128)S(1)} async-done(((f32[32,1,4096]{2,1,0:T(1,128)}), f32[32,1,4096]{2,1,0:T(1,128)S(1)}, u32[]{:S(2)}, u32[]{:S(2)}) %all-to-all-start.2) | async-done | bytes 524320 | tf_op jit(solution)/shard_map/all_to_all | solution.py:158
  149.2 3.6 collective-permute-start.2
  158.0 17.4 %multiply_add_fusion.20 = f32[1,32,1024]{2,1,0:T(8,128)S(1)} fusion(f32[1,32,1024]{2,1,0:T(8,128)S(1)} %squeeze.82, f32[3,34,1026]{2,1,0:T(8,128)S(1)} %select_maximum_fusion.20, f32[1,34,1024]{2,1,0:T(8,128)S(1)} %collective-permute-done.3, f32[1,34,1024]{2,1,0:T(8,128)S(1)} %collective-permute-done.2, f32[1,1,1024]{2,1,0:T(1,128)S(1)} %collective-permute-done, ...), kind=kLoop, calls=%fused_computation.485 | loop fusion | flops 1802240 | bytes 3416172 | tf_op jit(solution)/shard_map/add | solution.py:190
  182.6 3.9 collective-permute-start.6
  191.5 18.1 %multiply_reduce_fusion.88 = (f32[]{:T(128)}, f32[]{:T(128)}, f32[1,32,1024]{2,1,0:T(8,128)S(1)}) fusion(f32[1,32,1024]{2,1,0:T(8,128)S(1)} %squeeze.82, f32[1,32,1024]{2,1,0:T(8,128)S(1)} %squeeze.83, f32[3,34,1026]{2,1,0:T(8,128)S(1)} %select_maximum_fusion.16, f32[]{:T(128)} %bitcast.121, f32[1,34,1024]{2,1,0:T(8,128)S(1)} %collective-permute-done.7, ...), kind=kLoop, calls=%fused_computation.484 | loop fusion | flops 1966078 | bytes 3678324 | tf_op jit(solution)/shard_map/reduce_sum | solution.py:273
  212.5 28.8 %all-reduce.47 = (f32[16]{0:T(128)S(1)}, f32[16]{0:T(128)S(1)}) all-reduce(f32[16]{0:T(128)S(1)} %dynamic-update-slice, f32[16]{0:T(128)S(1)} %dynamic-update-slice.4), channel_id=1, replica_groups=mesh['gy_0'=16,'gy_1'=2,'gz_0'=4,'gz_1'=4] {'gy_0'}, use_global_device_ids=true, to_apply=%add.6 | all-reduce | flops 32 | bytes 256
  254.4 15.8 %all-reduce.53 = (f32[4]{0:T(128)S(1)}, f32[4]{0:T(128)S(1)}) all-reduce(f32[4]{0:T(128)S(1)} %dynamic-update-slice.2, f32[4]{0:T(128)S(1)} %dynamic-update-slice.6), channel_id=1, replica_groups=mesh['gy_0'=16,'gy_1'=2,'gz_0'=4,'gz_1'=4] {'gz_0'}, use_global_device_ids=true, to_apply=%add.8 | all-reduce | flops 8 | bytes 64
  273.9 9.8 %all-reduce.50 = (f32[4]{0:T(128)S(1)}, f32[4]{0:T(128)S(1)}) all-reduce(f32[4]{0:T(128)S(1)} %dynamic-update-slice.3, f32[4]{0:T(128)S(1)} %dynamic-update-slice.7), channel_id=1, replica_groups=mesh['gy_0'=16,'gy_1'=2,'gz_0'=4,'gz_1'=4] {'gz_1'}, use_global_device_ids=true, to_apply=%add.9 | all-reduce | flops 8 | bytes 64
  288.5 27.2 %all-reduce.14 = f32[16]{0:T(128)S(1)} all-reduce(f32[16]{0:T(128)S(1)} %dynamic-update-slice.8), channel_id=1, replica_groups=mesh['gy_0'=16,'gy_1'=2,'gz_0'=4,'gz_1'=4] {'gy_0'}, use_global_device_ids=true, to_apply=%add.14 | all-reduce | flops 16 | bytes 128
  322.1 7.7 all-reduce.16
  331.7 7.8 all-reduce.17
  346.4 8.0 all-to-all-start.3
  360.2 3.9 collective-permute-start.11
  366.3 11.0 %all-to-all-done.3 = f32[32,1,2048]{2,1,0:T(1,128)S(1)} async-done(((f32[32,1,2048]{2,1,0:T(1,128)}), f32[32,1,2048]{2,1,0:T(1,128)S(1)}, u32[]{:S(2)}, u32[]{:S(2)}) %all-to-all-start.3) | async-done | bytes 262176 | tf_op jit(solution)/shard_map/all_to_all | solution.py:105
  393.2 8.9 all-to-all-start.4
  402.4 17.4 %multiply_add_fusion.14 = f32[1,32,1024]{2,1,0:T(8,128)S(1)} fusion(f32[1,32,1024]{2,1,0:T(8,128)S(1)} %multiply_add_fusion.19, f32[3,34,1026]{2,1,0:T(8,128)S(1)} %select_maximum_fusion.12, f32[1,34,1024]{2,1,0:T(8,128)S(1)} %collective-permute-done.11, f32[1,34,1024]{2,1,0:T(8,128)S(1)} %collective-permute-done.10, ...), kind=kLoop, calls=%fused_computation.472 | loop fusion | flops 1802240 | bytes 3416172 | tf_op jit(solution)/shard_map/add | solution.py:190
  425.0 3.9 collective-permute-start.15
  433.7 4.1 collective-permute-done.14
  453.6 19.9 %multiply_reduce_fusion.86 = (f32[]{:T(128)}, f32[]{:T(128)}, f32[1,32,1024]{2,1,0:T(8,128)}) fusion(f32[1,32,1024]{2,1,0:T(8,128)S(1)} %multiply_add_fusion.19, f32[1,32,1024]{2,1,0:T(8,128)S(1)} %copy-done.11, f32[1,32,1024]{2,1,0:T(8,128)} %div.78, f32[3,34,1026]{2,1,0:T(8,128)S(1)} %select_maximum_fusion.8, f32[]{:T(128)} %bitcast.121, ...), kind=kLoop, calls=%fused_computation.471 | loop fusion | flops 1966078 | bytes 3809396 | tf_op jit(solution)/shard_map/reduce_sum | solution.py:273
  476.3 31.9 %all-reduce.46 = (f32[16]{0:T(128)S(1)}, f32[16]{0:T(128)S(1)}) all-reduce(f32[16]{0:T(128)S(1)} %dynamic-update-slice.16, f32[16]{0:T(128)S(1)} %dynamic-update-slice.12), channel_id=1, replica_groups=mesh['gy_0'=16,'gy_1'=2,'gz_0'=4,'gz_1'=4] {'gy_0'}, use_global_device_ids=true, to_apply=%add.22 | all-reduce | flops 32 | bytes 256
  520.1 10.1 %all-reduce.52 = (f32[4]{0:T(128)S(1)}, f32[4]{0:T(128)S(1)}) all-reduce(f32[4]{0:T(128)S(1)} %dynamic-update-slice.18, f32[4]{0:T(128)S(1)} %dynamic-update-slice.14), channel_id=1, replica_groups=mesh['gy_0'=16,'gy_1'=2,'gz_0'=4,'gz_1'=4] {'gz_0'}, use_global_device_ids=true, to_apply=%add.24 | all-reduce | flops 8 | bytes 64
  535.4 11.5 %all-reduce.49 = (f32[4]{0:T(128)S(1)}, f32[4]{0:T(128)S(1)}) all-reduce(f32[4]{0:T(128)S(1)} %dynamic-update-slice.19, f32[4]{0:T(128)S(1)} %dynamic-update-slice.15), channel_id=1, replica_groups=mesh['gy_0'=16,'gy_1'=2,'gz_0'=4,'gz_1'=4] {'gz_1'}, use_global_device_ids=true, to_apply=%add.25 | all-reduce | flops 8 | bytes 64
  555.1 29.9 %all-reduce.45 = (f32[16]{0:T(128)S(1)}, f32[16]{0:T(128)S(1)}, f32[16]{0:T(128)S(1)}, f32[16]{0:T(128)S(1)}) all-reduce(f32[16]{0:T(128)S(1)} %dynamic-update-slice.28, f32[16]{0:T(128)S(1)} %dynamic-update-slice.20, f32[16]{0:T(128)S(1)} %dynamic-update-slice.24, ...), channel_id=1, replica_groups=mesh['gy_0'=16,'gy_1'=2,'gz_0'=4,'gz_1'=4] {'gy_0'}, use_global_device_ids=true, to_apply=%add.34 | all-reduce | flops 64 | bytes 512
  603.4 8.6 all-reduce.51
  620.8 7.7 all-reduce.48
  635.8 7.9 all-to-all-start.5
  653.3 3.9 collective-permute-start.19
  659.2 7.4 all-to-all-done.5
  692.2 8.7 all-to-all-start.6
  701.2 18.9 %multiply_reduce_fusion.28 = (f32[]{:T(128)}, f32[]{:T(128)}, f32[]{:T(128)}, f32[]{:T(128)}, f32[]{:T(128)}, /*index=5*/f32[]{:T(128)}, f32[]{:T(128)}, f32[]{:...) fusion(f32[1,34,1024]{2,1,0:T(8,128)S(1)} %collective-permute-done.3, ...), kind=kLoop, calls=%fused_computation.391 | loop fusion | flops 2555895 | bytes 4604056 | tf_op jit(solution)/shard_map/reduce_sum | solution.py:208
  725.3 3.9 collective-permute-start.23
  734.6 3.6 collective-permute-done.22
  754.3 19.0 %fusion.91 = f32[4,8,8,128]{3,1,2,0:T(8,128)S(1)} fusion(f32[1,32,1024]{2,1,0:T(8,128)S(1)} %multiply_add_fusion.12, f32[1,32,1024]{2,1,0:T(8,128)} %div.87, f32[3,34,1026]{2,1,0:T(8,128)S(1)} %select_maximum_fusion, f32[1,34,1024]{2,1,0:T(8,128)} %copy-done.15, f32[1,1,1024]{2,1,0:T(1,128)S(1)} %collective-permute-done.21, f32[1,32,1024]{2,1,0:T(8,128)} %copy-done.10, ...), kind=kLoop, calls=%fused_computation.194 | loop fusion | flops 2162688 | bytes 4202620
  778.7 13.9 %all-to-all-start.7 = ((f32[32,1,2048]{2,1,0:T(1,128)}), f32[32,1,2048]{2,1,0:T(1,128)S(1)}, u32[]{:S(2)}, u32[]{:S(2)}) async-start(f32[32,1,2048]{2,1,0:T(1,128)} %reshape.2688), calls=%async_computation.7 | async-start | bytes 524288 | tf_op jit(solution)/shard_map/all_to_all | solution.py:105
  795.6 19.7 %all-to-all-done.7 = f32[32,1,2048]{2,1,0:T(1,128)S(1)} async-done(((f32[32,1,2048]{2,1,0:T(1,128)}), f32[32,1,2048]{2,1,0:T(1,128)S(1)}, u32[]{:S(2)}, u32[]{:S(2)}) %all-to-all-start.7) | async-done | bytes 262176 | tf_op jit(solution)/shard_map/all_to_all | solution.py:105
  844.3 3.9 all-to-all-start.8
  849.1 16.9 %stack.528 = f32[1,27]{1,0:T(1,128)S(1)} concatenate(f32[1,1]{1,0:T(1,128)} %bitcast.345, f32[1,1]{1,0:T(1,128)} %bitcast.346, f32[1,1]{1,0:T(1,128)} %bitcast.347, f32[1,1]{1,0:T(1,128)} %bitcast.348, f32[1,1]{1,0:T(1,128)} %bitcast.349, f32[1,1]{1,0:T(1,128)} %bitcast.350, f32[1,1]{1,0:T(1,128)} %bitcast.351, f32[1,1]{1,0:T(1,128)} %bitcast.352, f32[1,1]{1,0:T(1,128)} %bitcast.353, ...), dimensions={1} | concatenate | bytes 216 | tf_op jit(solution)/shard_map/stack | solution.py:217
  867.2 16.9 %stack.556 = f32[1,27]{1,0:T(1,128)S(1)} concatenate(f32[1,1]{1,0:T(1,128)} %bitcast.372, f32[1,1]{1,0:T(1,128)} %bitcast.373, f32[1,1]{1,0:T(1,128)} %bitcast.374, f32[1,1]{1,0:T(1,128)} %bitcast.375, f32[1,1]{1,0:T(1,128)} %bitcast.376, f32[1,1]{1,0:T(1,128)} %bitcast.377, f32[1,1]{1,0:T(1,128)} %bitcast.378, f32[1,1]{1,0:T(1,128)} %bitcast.379, f32[1,1]{1,0:T(1,128)} %bitcast.380, ...), dimensions={1} | concatenate | bytes 216 | tf_op jit(solution)/shard_map/stack | solution.py:217
  886.1 17.2 %stack.584 = f32[1,27]{1,0:T(1,128)S(1)} concatenate(f32[1,1]{1,0:T(1,128)} %bitcast.399, f32[1,1]{1,0:T(1,128)} %bitcast.400, f32[1,1]{1,0:T(1,128)} %bitcast.401, f32[1,1]{1,0:T(1,128)} %bitcast.402, f32[1,1]{1,0:T(1,128)} %bitcast.403, f32[1,1]{1,0:T(1,128)} %bitcast.404, f32[1,1]{1,0:T(1,128)} %bitcast.405, f32[1,1]{1,0:T(1,128)} %bitcast.406, f32[1,1]{1,0:T(1,128)} %bitcast.407, ...), dimensions={1} | concatenate | bytes 216 | tf_op jit(solution)/shard_map/stack | solution.py:217
  903.3 29.6 %all-gather.3 = f32[16,1,27]{2,1,0:T(1,128)S(1)} all-gather(f32[1,1,27]{2,1,0:T(1,128)S(1)} %add_bitcast_fusion.1), channel_id=1, replica_groups=mesh['gy_0'=16,'gy_1'=2,'gz_0'=4,'gz_1'=4] {'gy_0'}, dimensions={0}, use_global_device_ids=true | all-gather | bytes 1836 | tf_op jit(solution)/shard_map/all_gather | solution.py:30
  936.0 9.3 all-reduce.43
  945.6 11.8 %all-reduce.44 = f32[108]{0:T(128)S(1)} all-reduce(f32[108]{0:T(128)S(1)} %dynamic-update-slice.38), channel_id=4, replica_groups=mesh['gy_0'=16,'gy_1'=2,'gz_0'=4,'gz_1'=4] {'gz_1'}, use_global_device_ids=true, to_apply=%add.44 | all-reduce | flops 108 | bytes 864
  (437 shorter events, 320.1 us)
Async XLA Ops:
  6.9 38.2 %all-to-all-start.1 = ((f32[32,1,2048]{2,1,0:T(1,128)}), f32[32,1,2048]{2,1,0:T(1,128)S(1)}, u32[]{:S(2)}, u32[]{:S(2)}) async-start(f32[32,1,2048]{2,1,0:T(1,128)} %reshape.2676), calls=%async_computation.1 | async-start | bytes 524288 | tf_op jit(solution)/shard_map/all_to_all | solution.py:105
  45.2 26.7 %all-to-all-start = ((f32[32,1,2048]{2,1,0:T(1,128)}), f32[32,1,2048]{2,1,0:T(1,128)S(1)}, u32[]{:S(2)}, u32[]{:S(2)}) async-start(f32[32,1,2048]{2,1,0:T(1,128)} %reshape.2674), calls=%async_computation | async-start | bytes 524288 | tf_op jit(solution)/shard_map/all_to_all | solution.py:105
  77.7 308.0 %copy-start.12 = (f32[32,8,128]{2,0,1:T(8,128)}, f32[32,8,128]{2,0,1:T(8,128)S(1)}, u32[]{:S(2)}) copy-start(f32[32,8,128]{2,0,1:T(8,128)S(1)} %get-tuple-element.202) | copy-start | bytes 393220
  92.0 37.9 %all-to-all-start.2 = ((f32[32,1,4096]{2,1,0:T(1,128)}), f32[32,1,4096]{2,1,0:T(1,128)S(1)}, u32[]{:S(2)}, u32[]{:S(2)}) async-start(f32[32,1,4096]{2,1,0:T(1,128)} %reshape.2678), calls=%async_computation.2 | async-start | bytes 1048576 | tf_op jit(solution)/shard_map/all_to_all | solution.py:158
  141.6 4.3 collective-permute-start.1
  142.9 3.8 collective-permute-start
  146.8 8.9 collective-permute-start.3
  149.2 8.6 collective-permute-start.2
  175.5 4.3 collective-permute-start.5
  176.8 3.8 collective-permute-start.4
  180.6 8.7 collective-permute-start.7
  182.6 8.7 collective-permute-start.6
  191.5 94.8 %copy-start.11 = (f32[1,32,1024]{2,1,0:T(8,128)S(1)}, f32[1,32,1024]{2,1,0:T(8,128)}, u32[]{:S(2)}) copy-start(f32[1,32,1024]{2,1,0:T(8,128)} %param.7) | copy-start | bytes 393220
  209.6 420.8 %copy-start.4 = (f32[1,32,1024]{2,1,0:T(8,128)}, f32[1,32,1024]{2,1,0:T(8,128)S(1)}, u32[]{:S(2)}) copy-start(f32[1,32,1024]{2,1,0:T(8,128)S(1)} %get-tuple-element.146) | copy-start | bytes 393220
  346.4 30.9 %all-to-all-start.3 = ((f32[32,1,2048]{2,1,0:T(1,128)}), f32[32,1,2048]{2,1,0:T(1,128)S(1)}, u32[]{:S(2)}, u32[]{:S(2)}) async-start(f32[32,1,2048]{2,1,0:T(1,128)} %reshape.2680), calls=%async_computation.3 | async-start | bytes 524288 | tf_op jit(solution)/shard_map/all_to_all | solution.py:105
  354.4 4.3 collective-permute-start.9
  355.7 3.8 collective-permute-start.8
  358.7 43.6 %copy-start.19 = (f32[1,1,1024]{2,1,0:T(1,128)}, f32[1,1,1024]{2,1,0:T(1,128)S(1)}, u32[]{:S(2)}) copy-start(f32[1,1,1024]{2,1,0:T(1,128)S(1)} %collective-permute-done.9) | copy-start | bytes 12292
  359.5 42.9 %copy-start.21 = (f32[1,1,1024]{2,1,0:T(1,128)}, f32[1,1,1024]{2,1,0:T(1,128)S(1)}, u32[]{:S(2)}) copy-start(f32[1,1,1024]{2,1,0:T(1,128)S(1)} %collective-permute-done.8) | copy-start | bytes 12292
  360.2 41.9 %collective-permute-start.11 = (f32[1,34,1024]{2,1,0:T(8,128)}, f32[1,34,1024]{2,1,0:T(8,128)S(1)}, u32[]{:S(2)}, u32[]{:S(2)}) collective-permute-start(f32[1,34,1024]{2,1,0:T(8,128)} %pad_maximum_fusion.3), channel_id=1, source_target_pairs={{1,0},{2,1},{3,2},{4,3},{5,4},{6,5},{7,6},{8,7},{9,8},{10,9},{11,1... | collective-permute-start | bytes 417800 | tf_op jit(solution)/shard_map/ppermute | solution.py:23
  364.2 38.0 %collective-permute-start.10 = (f32[1,34,1024]{2,1,0:T(8,128)}, f32[1,34,1024]{2,1,0:T(8,128)S(1)}, u32[]{:S(2)}, u32[]{:S(2)}) collective-permute-start(f32[1,34,1024]{2,1,0:T(8,128)} %pad_maximum_fusion.3), channel_id=1, source_target_pairs={{0,1},{1,2},{2,3},{3,4},{4,5},{5,6},{6,7},{7,8},{8,9},{9,10},{10,1... | collective-permute-start | bytes 417800 | tf_op jit(solution)/shard_map/ppermute | solution.py:22
  393.2 45.5 %all-to-all-start.4 = ((f32[32,1,2048]{2,1,0:T(1,128)}), f32[32,1,2048]{2,1,0:T(1,128)}, u32[]{:S(2)}, u32[]{:S(2)}) async-start(f32[32,1,2048]{2,1,0:T(1,128)} %reshape.2682), calls=%async_computation.4 | async-start | bytes 524288 | tf_op jit(solution)/shard_map/all_to_all | solution.py:158
  402.1 17.7 %copy-start = (f32[1,34,1024]{2,1,0:T(8,128)}, f32[1,34,1024]{2,1,0:T(8,128)S(1)}, u32[]{:S(2)}) copy-start(f32[1,34,1024]{2,1,0:T(8,128)S(1)} %collective-permute-done.10) | copy-start | bytes 417796
  419.8 33.7 %copy-start.2 = (f32[1,32,1024]{2,1,0:T(8,128)}, f32[1,32,1024]{2,1,0:T(8,128)S(1)}, u32[]{:S(2)}) copy-start(f32[1,32,1024]{2,1,0:T(8,128)S(1)} %multiply_add_fusion.14) | copy-start | bytes 393220
  419.8 4.3 collective-permute-start.13
  421.1 3.8 collective-permute-start.12
  425.0 8.7 collective-permute-start.15
  428.9 8.8 collective-permute-start.14
  552.2 80.5 %copy-start.16 = (f32[1,32,1024]{2,1,0:T(8,128)}, f32[1,32,1024]{2,1,0:T(8,128)S(1)}, u32[]{:S(2)}) copy-start(f32[1,32,1024]{2,1,0:T(8,128)S(1)} %get-tuple-element.144) | copy-start | bytes 393220
  635.8 30.8 %all-to-all-start.5 = ((f32[32,1,2048]{2,1,0:T(1,128)}), f32[32,1,2048]{2,1,0:T(1,128)S(1)}, u32[]{:S(2)}, u32[]{:S(2)}) async-start(f32[32,1,2048]{2,1,0:T(1,128)} %reshape.2684), calls=%async_computation.5 | async-start | bytes 524288 | tf_op jit(solution)/shard_map/all_to_all | solution.py:105
  643.7 8.9 collective-permute-start.17
  645.0 7.6 collective-permute-start.16
  652.6 48.6 %copy-start.23 = (f32[1,1,1024]{2,1,0:T(1,128)}, f32[1,1,1024]{2,1,0:T(1,128)S(1)}, u32[]{:S(2)}) copy-start(f32[1,1,1024]{2,1,0:T(1,128)S(1)} %collective-permute-done.17) | copy-start | bytes 12292
  652.6 48.6 %copy-start.25 = (f32[1,1,1024]{2,1,0:T(1,128)}, f32[1,1,1024]{2,1,0:T(1,128)S(1)}, u32[]{:S(2)}) copy-start(f32[1,1,1024]{2,1,0:T(1,128)S(1)} %collective-permute-done.16) | copy-start | bytes 12292
  653.3 47.6 %collective-permute-start.19 = (f32[1,34,1024]{2,1,0:T(8,128)}, f32[1,34,1024]{2,1,0:T(8,128)S(1)}, u32[]{:S(2)}, u32[]{:S(2)}) collective-permute-start(f32[1,34,1024]{2,1,0:T(8,128)} %pad_maximum_fusion.5), channel_id=1, source_target_pairs={{1,0},{2,1},{3,2},{4,3},{5,4},{6,5},{7,6},{8,7},{9,8},{10,9},{11,1... | collective-permute-start | bytes 417800 | tf_op jit(solution)/shard_map/ppermute | solution.py:23
  657.2 43.7 %collective-permute-start.18 = (f32[1,34,1024]{2,1,0:T(8,128)}, f32[1,34,1024]{2,1,0:T(8,128)S(1)}, u32[]{:S(2)}, u32[]{:S(2)}) collective-permute-start(f32[1,34,1024]{2,1,0:T(8,128)} %pad_maximum_fusion.5), channel_id=1, source_target_pairs={{0,1},{1,2},{2,3},{3,4},{4,5},{5,6},{6,7},{7,8},{8,9},{9,10},{10,1... | collective-permute-start | bytes 417800 | tf_op jit(solution)/shard_map/ppermute | solution.py:22
  692.2 47.3 %all-to-all-start.6 = ((f32[32,1,2048]{2,1,0:T(1,128)}), f32[32,1,2048]{2,1,0:T(1,128)}, u32[]{:S(2)}, u32[]{:S(2)}) async-start(f32[32,1,2048]{2,1,0:T(1,128)} %reshape.2686), calls=%async_computation.6 | async-start | bytes 524288 | tf_op jit(solution)/shard_map/all_to_all | solution.py:158
  720.1 13.8 %copy-start.10 = (f32[1,32,1024]{2,1,0:T(8,128)}, f32[1,32,1024]{2,1,0:T(8,128)S(1)}, u32[]{:S(2)}) copy-start(f32[1,32,1024]{2,1,0:T(8,128)S(1)} %get-tuple-element.143) | copy-start | bytes 393220
  720.1 4.3 collective-permute-start.21
  721.4 3.8 collective-permute-start.20
  725.3 8.7 collective-permute-start.23
  729.2 9.0 collective-permute-start.22
  773.8 20.7 %copy-start.3 = (f32[1,32,1024]{2,1,0:T(8,128)S(1)}, f32[1,32,1024]{2,1,0:T(8,128)}, u32[]{:S(2)}) copy-start(f32[1,32,1024]{2,1,0:T(8,128)} %copy-done.2) | copy-start | bytes 393220
  778.7 36.7 %all-to-all-start.7 = ((f32[32,1,2048]{2,1,0:T(1,128)}), f32[32,1,2048]{2,1,0:T(1,128)S(1)}, u32[]{:S(2)}, u32[]{:S(2)}) async-start(f32[32,1,2048]{2,1,0:T(1,128)} %reshape.2688), calls=%async_computation.7 | async-start | bytes 524288 | tf_op jit(solution)/shard_map/all_to_all | solution.py:105
  841.3 24.8 %copy-start.17 = (f32[1,32,1024]{2,1,0:T(8,128)S(1)}, f32[1,32,1024]{2,1,0:T(8,128)}, u32[]{:S(2)}) copy-start(f32[1,32,1024]{2,1,0:T(8,128)} %get-tuple-element.142) | copy-start | bytes 393220
  844.3 113.9 %all-to-all-start.8 = ((f32[32,1,2048]{2,1,0:T(1,128)}), f32[32,1,2048]{2,1,0:T(1,128)S(1)}, u32[]{:S(2)}, u32[]{:S(2)}) async-start(f32[32,1,2048]{2,1,0:T(1,128)} %reshape.2690), calls=%async_computation.8 | async-start | bytes 524288 | tf_op jit(solution)/shard_map/all_to_all | solution.py:158
  848.2 35.9 %copy-start.24 = (f32[1,1,1024]{2,1,0:T(1,128)S(1)}, f32[1,1,1024]{2,1,0:T(1,128)}, u32[]{:S(2)}) copy-start(f32[1,1,1024]{2,1,0:T(1,128)} %copy-done.23) | copy-start | bytes 12292
  848.2 35.9 %copy-start.26 = (f32[1,1,1024]{2,1,0:T(1,128)S(1)}, f32[1,1,1024]{2,1,0:T(1,128)}, u32[]{:S(2)}) copy-start(f32[1,1,1024]{2,1,0:T(1,128)} %copy-done.25) | copy-start | bytes 12292
  (13 other events, 72.9 us)
